TPU v7x, 256 devices: a whole 4x4x8 slice. The times are simulated.
256 devices in a mesh: dp: 16 (over z, core), mp: 16 (over x, y).
Axes of the slice: x: 4, y: 4, z: 8, core: 2. Of those that a mesh axis runs over, the one named last changes fastest.
Arguments:
- hidden_in: bfloat16 [64, 64, 7168], P('dp', None, 'mp'), may hold values from -6 to 6
- norm_gain: bfloat16 [7168], P('mp'), may hold values from 0.099609375 to 1.8984375
- w_query: bfloat16 [7168, 7168], P('dp', 'mp'), may hold values from -0.070868339 to 0.070868339
- w_key: bfloat16 [7168, 1024], P('dp', 'mp'), may hold values from -0.070868339 to 0.070868339
- w_value: bfloat16 [7168, 1024], P('dp', 'mp'), may hold values from -0.0625 to 0.0625
- w_out: bfloat16 [7168, 7168], P('mp', 'dp'), may hold values from -0.09375 to 0.09375
- key_cache: bfloat16 [64, 16, 1, 2048, 128], P('dp', 'mp'), may hold values from -52 to 52
- value_cache: bfloat16 [64, 16, 1, 2048, 128], P('dp', 'mp'), may hold values from -3 to 3
- cache_len: int32 [64], P('dp'), may hold values from 256 to 4096, as said below
- tree_parent: int32 [64, 64], P('dp'), may hold values from 0 to 62, as said below
- valid_nodes: int32 [64, 64], P('dp'), may hold values from 0 to 1, as said below
- accepted_path: int32 [64, 8], P('dp'), may hold values from 0 to 63, as said below
- slot_owner: int32 [64], replicated, may hold values from 0 to 63, each once
Outputs:
- layer_out: bfloat16 [64, 64, 7168], P('dp', None, 'mp')
- accepted_kv: bfloat16 [64, 8, 2, 1024], P('dp', None, None, 'mp')
Inputs may be any that keep to these rules, and one draw needn't show every extreme that they name: `cache_len`: some request holds exactly 4096 positions in every draw. `tree_parent`: node 0 is its own parent; every other node's parent is one of the three nodes before it. `valid_nodes`: the 1 entries of each request form a prefix of 32 to 64 nodes. `accepted_path`: each row is a chain in which every node is the parent of the next (node 0 may repeat at the start), ending at the request's last real node. `slot_owner`: each slot is named once.
All inputs are finite; a program needn't handle non-finite values.
Results may differ from a plain program's by a relative error of at most 0.007.
The roundings to bfloat16 on the way count: a program that leaves them out, or rounds other values in their place, can miss the bound.
Values may be sent and summed in bfloat16 or wider, within the bound.
No kernel may reach another device: no remote copies, remote signals or barrier semaphores. Data moves between devices by JAX's collectives and lax.ppermute only.
A program may use at most 128 MiB of HBM per device.

v0:
```python
import math

import jax
import jax.numpy as jnp
from jax import lax
from jax.sharding import PartitionSpec as P

GROUP = 7


epsilon = 1e-05
rope_base = 5000000.0
masked_score = -1e30


def from_partner(block, axis, stride):
    count = lax.axis_size(axis)
    route = []
    for low in range(count):
        high = low | 1 << stride
        if high != low and high < count:
            route += [(low, high), (high, low)]
    return lax.ppermute(block, axis, route)


def tree_closure(parents):
    width = parents.shape[-1]
    nodes = jnp.arange(width, dtype=jnp.int32)
    onehot = (parents[..., None] == nodes).astype(jnp.float32)
    reach = jnp.minimum(jnp.eye(width, dtype=jnp.float32) + onehot, 1.0)
    for rounds in range((width - 1).bit_length()):
        reach = jnp.minimum(
            jnp.einsum("rij,rjk->rik", reach, reach, precision=lax.Precision.HIGHEST), 1.0
        )
    return reach


def rotate(values, positions):
    head_dim = values.shape[-1]
    half_dim = head_dim // 2
    freq_steps = jnp.arange(half_dim, dtype=jnp.float32)
    inverse = jnp.exp(freq_steps * (-2.0 * math.log(rope_base) / head_dim))
    angles = positions[..., None] * inverse
    cosine = jnp.concatenate([jnp.cos(angles), jnp.cos(angles)], -1)[..., None, :]
    sine = jnp.concatenate([jnp.sin(angles), jnp.sin(angles)], -1)[..., None, :]
    turned = jnp.concatenate([-values[..., half_dim:], values[..., :half_dim]], -1)
    return values * cosine + turned * sine


def shards(
    hidden_in,
    norm_gain,
    w_query,
    w_key,
    w_value,
    w_out,
    key_cache,
    value_cache,
    cache_len,
    tree_parent,
    valid_nodes,
    accepted_path,
    slot_owner,
):
    req_dev, tree_size, part_width = hidden_in.shape
    row_count = req_dev * tree_size
    head_dim = key_cache.shape[-1]
    half_len = key_cache.shape[3]
    kv_group = key_cache.shape[2]
    q_cols = w_query.shape[1]
    k_cols = w_key.shape[1]
    gathered, full_gain = (
        lax.all_gather(hidden_in, "mp", axis=2, tiled=True),
        lax.all_gather(norm_gain, "mp", axis=0, tiled=True),
    )
    widened = gathered.astype(jnp.float32)
    meansq = jnp.mean(widened * widened, -1, keepdims=True)
    normed = (widened * lax.rsqrt(meansq + epsilon) * full_gain.astype(jnp.float32)).astype(
        jnp.bfloat16
    )
    flat = normed.reshape(row_count, gathered.shape[2])
    pieces = (
        lax.all_gather(w_query, "dp", axis=0, tiled=True),
        lax.all_gather(w_key, "dp", axis=0, tiled=True),
        lax.all_gather(w_value, "dp", axis=0, tiled=True),
    )
    query_sum, key_sum, value_sum = tuple(
        (jnp.dot(flat, piece, preferred_element_type=jnp.float32) for piece in pieces)
    )
    query = query_sum.astype(jnp.bfloat16)
    key_new = key_sum.astype(jnp.bfloat16)
    value_new = value_sum.astype(jnp.bfloat16)
    other_query, other_key, other_value = from_partner((query, key_new, value_new), "mp", 0)
    half_index = lax.axis_index("mp") % 2
    is_first = half_index == 0

    def paired(own_part, other_part):
        return jnp.where(
            is_first,
            jnp.concatenate([own_part, other_part], 1),
            jnp.concatenate([other_part, own_part], 1),
        )

    group_query = paired(query, other_query)
    group_key = paired(key_new, other_key)
    group_value = paired(value_new, other_value)
    reach = tree_closure(tree_parent)
    depth = jnp.sum(reach, -1) - 1.0
    position = cache_len[:, None].astype(jnp.float32) + depth
    rot_query = rotate(
        group_query.reshape(req_dev, tree_size, kv_group * GROUP, head_dim).astype(jnp.float32),
        position,
    ).astype(jnp.bfloat16)
    rot_key = rotate(
        group_key.reshape(req_dev, tree_size, kv_group, head_dim).astype(jnp.float32), position
    ).astype(jnp.bfloat16)
    node_values = group_value.reshape(req_dev, tree_size, kv_group, head_dim)
    queries_all = (
        rot_query.reshape(req_dev, tree_size, kv_group, GROUP, head_dim)
        .transpose(0, 2, 3, 1, 4)
        .reshape(req_dev, kv_group, GROUP * tree_size, head_dim)
    )
    scale = 1.0 / math.sqrt(head_dim)

    def one_request(packed):
        queries, key_r, value_r, cached_keys, cached_values, length, reach_r = packed
        tree_keys = key_r.transpose(1, 0, 2)
        tree_values = value_r.transpose(1, 0, 2)
        count = jnp.clip(length - half_index * half_len, 0, half_len)
        scores_tree = (
            jnp.einsum("gqd,gkd->gqk", queries, tree_keys, preferred_element_type=jnp.float32)
            * scale
        )
        tiled = jnp.logical_and(jnp.tile(reach_r, (GROUP, 1)) > 0.5, is_first)
        scores_tree = jnp.where(tiled[None], scores_tree, masked_score)
        scores_cache = (
            jnp.einsum("gqd,gkd->gqk", queries, cached_keys, preferred_element_type=jnp.float32)
            * scale
        )
        live = jnp.arange(half_len, dtype=jnp.int32) < count
        scores_cache = jnp.where(live[None, None, :], scores_cache, masked_score)
        highest = jnp.maximum(jnp.max(scores_cache, -1), jnp.max(scores_tree, -1))
        probs_cache = jnp.exp(scores_cache - highest[..., None]).astype(jnp.bfloat16)
        probs_tree = jnp.exp(scores_tree - highest[..., None]).astype(jnp.bfloat16)
        totals = jnp.sum(probs_cache.astype(jnp.float32), -1) + jnp.sum(
            probs_tree.astype(jnp.float32), -1
        )
        weighted = jnp.einsum(
            "gqk,gkd->gqd", probs_cache, cached_values, preferred_element_type=jnp.float32
        )
        weighted = weighted + jnp.einsum(
            "gqk,gkd->gqd", probs_tree, tree_values, preferred_element_type=jnp.float32
        )
        return (highest, totals, weighted)

    highest, totals, weighted = lax.map(
        one_request,
        (queries_all, rot_key, node_values, key_cache[:, 0], value_cache[:, 0], cache_len, reach),
    )
    other_high, other_totals, other_weighted = from_partner((highest, totals, weighted), "mp", 0)
    ceiling = jnp.maximum(highest, other_high)
    own_factor = jnp.exp(highest - ceiling)
    other_factor = jnp.exp(other_high - ceiling)
    numerator = weighted * own_factor[..., None] + other_weighted * other_factor[..., None]
    denominator = totals * own_factor + other_totals * other_factor
    attended = (numerator / denominator[..., None]).astype(jnp.bfloat16)
    attended = (
        attended.reshape(req_dev, kv_group, GROUP, tree_size, head_dim)
        .transpose(0, 3, 1, 2, 4)
        .reshape(req_dev, tree_size, kv_group * GROUP * head_dim)
    )
    attended = attended * valid_nodes[..., None].astype(jnp.bfloat16)
    own_heads = lax.dynamic_slice_in_dim(
        attended.reshape(row_count, 2 * q_cols), half_index * q_cols, q_cols, 1
    )
    terms = jnp.dot(
        own_heads,
        lax.all_gather(w_out, "dp", axis=1, tiled=True),
        preferred_element_type=jnp.float32,
    )
    mine = lax.psum_scatter(terms, "mp", scatter_dimension=1, tiled=True)
    layer_out = (
        (hidden_in.reshape(row_count, part_width).astype(jnp.float32) + mine)
        .astype(jnp.bfloat16)
        .reshape(req_dev, tree_size, part_width)
    )
    own_keys = lax.dynamic_slice_in_dim(
        rot_key.reshape(req_dev, tree_size, kv_group * head_dim), half_index * k_cols, k_cols, 2
    )
    kv_rows = jnp.stack([own_keys, value_new.reshape(req_dev, tree_size, k_cols)], 2)
    chosen = jax.vmap(lambda rows_of, picks: jnp.take(rows_of, picks, axis=0))(
        kv_rows, accepted_path
    )
    every_row = lax.all_gather(chosen, "dp", axis=0, tiled=True)
    total_reqs = slot_owner.shape[0]
    my_slots = lax.axis_index("dp") * req_dev + jnp.arange(req_dev, dtype=jnp.int32)
    matches = slot_owner[None, :] == my_slots[:, None]
    senders = jnp.sum(jnp.where(matches, jnp.arange(total_reqs, dtype=jnp.int32)[None, :], 0), 1)
    accepted_kv = jnp.take(every_row, senders, axis=0)
    return (layer_out, accepted_kv)


def solution(mesh):
    placed = (
        P("dp", None, "mp"),
        P("mp"),
        P("dp", "mp"),
        P("dp", "mp"),
        P("dp", "mp"),
        P("mp", "dp"),
        P("dp", "mp", None, None, None),
        P("dp", "mp", None, None, None),
        P("dp"),
        P("dp", None),
        P("dp", None),
        P("dp", None),
        P(),
    )
    return jax.shard_map(
        shards,
        mesh=mesh,
        in_specs=placed,
        out_specs=(P("dp", None, "mp"), P("dp", None, None, "mp")),
        check_vma=False,
    )
```

profile of v0, /device:TPU:6, one launch (start us, length us, event | category | flops | bytes accessed | tf_op | source)
XLA Modules:
  0.0 352.1 jit_solution(6628368691060993493)
XLA Ops:
  7.2 2.0 copy.134
  10.1 2.0 copy.158
  12.2 1.3 dynamic-slice.1
  14.1 0.9 dynamic-update-slice
  15.0 68.0 %all-reduce = bf16[7168]{0:T(1024)(128)(2,1)S(1)} all-reduce(bf16[7168]{0:T(1024)(128)(2,1)S(1)} %dynamic-update-slice), channel_id=1, replica_groups=mesh['dp'=16,'mp'=16] {'mp'}, use_global_device_ids=true, to_apply=%add | all-reduce | flops 7168 | bytes 28672
  83.1 25.8 %all-gather = bf16[16,448,64]{1,2,0:T(8,128)(2,1)S(1)} all-gather(bf16[1,448,64]{1,2,0:T(8,128)(2,1)} %bitcast.153), channel_id=1, replica_groups=mesh['dp'=16,'mp'=16] {'dp'}, dimensions={0}, use_global_device_ids=true | all-gather | bytes 974848 | tf_op jit(solution)/shard_map/all_gather | solution.py:84
  109.4 1.2 reshape.579
  112.4 23.8 %all-gather.1 = bf16[16,448,64]{1,2,0:T(8,128)(2,1)S(1)} all-gather(bf16[1,448,64]{1,2,0:T(8,128)(2,1)S(1)} %bitcast.154), channel_id=1, replica_groups=mesh['dp'=16,'mp'=16] {'dp'}, dimensions={0}, use_global_device_ids=true | all-gather | bytes 974848 | tf_op jit(solution)/shard_map/all_gather | solution.py:85
  136.8 1.2 reshape.581
  138.6 0.8 pad_maximum_fusion
  139.4 11.3 %copy.135 = bf16[4,64,7168]{2,1,0:T(8,128)(2,1)} copy(bf16[4,64,7168]{1,0,2:T(4,128)(2,1)} %all-gather.6.cloned.1.call-done) | data formatting | bytes 7340032 | tf_op jit(solution)/shard_map/all_gather | solution.py:73
  150.7 3.0 fusion.22
  153.9 1.0 fusion.24
  154.9 1.2 convolution_convert_fusion.2
  156.2 0.9 collective-permute-start.1
  157.1 1.2 convolution_convert_fusion.1
  158.5 1.5 collective-permute-start.2
  160.7 7.1 %convolution_convert_fusion = bf16[256,448]{0,1:T(8,128)(2,1)S(1)} fusion(bf16[256,7168]{1,0:T(8,128)(2,1)} %bitcast.138, bf16[7168,448]{1,0:T(8,128)(2,1)} %all-gather.8.cloned.1.call-done), kind=kOutput, calls=%fused_computation.41 | convolution fusion | flops 1644281856 | bytes 10321920 | tf_op jit(solution)/shard_map/dot_general | solution.py:88
  167.8 0.9 collective-permute-start
  170.0 5.2 %collective-permute-done = bf16[256,448]{0,1:T(8,128)(2,1)S(1)} collective-permute-done((bf16[256,448]{0,1:T(8,128)(2,1)S(1)}, bf16[256,448]{0,1:T(8,128)(2,1)S(1)}, u32[]{:S(2)}, u32[]{:S(2)}) %collective-permute-start) | collective-permute-done | bytes 229408 | tf_op jit(solution)/shard_map/ppermute | solution.py:23
  177.4 42.4 %while.16 = (s32[]{:T(128)}, f32[4,1,448]{2,1,0:T(1,128)S(1)}, f32[4,1,448]{2,1,0:T(1,128)S(1)}, f32[4,1,448,128]{3,2,1,0:T(8,128)S(1)}, s32[4]{0:T(128)S(1)}, /...) while((s32[]{:T(128)}, f32[4,1,448]{2,1,0:T(1,128)S(1)}, ...), condition=%wide.region_7.8_spmd, body=%wide.region_2.7_spmd.sunk | while | flops 496694400 | bytes 28287568 | solution.py:156
  178.6 3.6 %fusion.79 = (f32[448]{0:T(512)S(1)}, f32[448,2048]{1,0:T(8,128)}) fusion(pred[2048]{0:T(1024)(128)(4,1)S(1)} %iota_compare_fusion.5, bf16[4,1,2048,128]{3,2,1,0:T(8,128)(2,1)} %get-tuple-element.394, s32[]{:T(128)} %get-tuple-element.371, bf16[4,1,448,128]{3,2,1,0:T(8,128)(2,1)S(1)} %get-tuple-element.393), kind=kOutput, calls=%fused_computation.5.clone.1 | convolution fusion | flops 237633088 | bytes 4313856 | tf_op jit(solution)/shard_map/while/body/eval_jaxpr/gqd,gkd->gqk/dot_general | solution.py:137
  182.8 1.1 fusion.81
  183.9 3.2 fusion.82
  187.2 0.8 convert_reduce_fusion.4
  189.3 3.6 %fusion.79 = (f32[448]{0:T(512)S(1)}, f32[448,2048]{1,0:T(8,128)}) fusion(pred[2048]{0:T(1024)(128)(4,1)S(1)} %iota_compare_fusion.5, bf16[4,1,2048,128]{3,2,1,0:T(8,128)(2,1)} %get-tuple-element.394, s32[]{:T(128)} %get-tuple-element.371, bf16[4,1,448,128]{3,2,1,0:T(8,128)(2,1)S(1)} %get-tuple-element.393), kind=kOutput, calls=%fused_computation.5.clone.1 | convolution fusion | flops 237633088 | bytes 4313856 | tf_op jit(solution)/shard_map/while/body/eval_jaxpr/gqd,gkd->gqk/dot_general | solution.py:137
  193.5 1.1 fusion.81
  194.6 3.1 fusion.82
  197.8 0.8 convert_reduce_fusion.4
  199.9 3.6 %fusion.79 = (f32[448]{0:T(512)S(1)}, f32[448,2048]{1,0:T(8,128)}) fusion(pred[2048]{0:T(1024)(128)(4,1)S(1)} %iota_compare_fusion.5, bf16[4,1,2048,128]{3,2,1,0:T(8,128)(2,1)} %get-tuple-element.394, s32[]{:T(128)} %get-tuple-element.371, bf16[4,1,448,128]{3,2,1,0:T(8,128)(2,1)S(1)} %get-tuple-element.393), kind=kOutput, calls=%fused_computation.5.clone.1 | convolution fusion | flops 237633088 | bytes 4313856 | tf_op jit(solution)/shard_map/while/body/eval_jaxpr/gqd,gkd->gqk/dot_general | solution.py:137
  204.1 1.1 fusion.81
  205.2 3.1 fusion.82
  208.3 0.8 convert_reduce_fusion.4
  210.5 3.6 %fusion.79 = (f32[448]{0:T(512)S(1)}, f32[448,2048]{1,0:T(8,128)}) fusion(pred[2048]{0:T(1024)(128)(4,1)S(1)} %iota_compare_fusion.5, bf16[4,1,2048,128]{3,2,1,0:T(8,128)(2,1)} %get-tuple-element.394, s32[]{:T(128)} %get-tuple-element.371, bf16[4,1,448,128]{3,2,1,0:T(8,128)(2,1)S(1)} %get-tuple-element.393), kind=kOutput, calls=%fused_computation.5.clone.1 | convolution fusion | flops 237633088 | bytes 4313856 | tf_op jit(solution)/shard_map/while/body/eval_jaxpr/gqd,gkd->gqk/dot_general | solution.py:137
  214.6 1.1 fusion.81
  215.8 3.1 fusion.82
  218.9 0.8 convert_reduce_fusion.4
  219.8 0.9 collective-permute-start.4
  220.6 1.3 collective-permute-start.3
  221.9 0.8 collective-permute-start.5
  222.7 18.5 %collective-permute-done.3 = f32[4,1,448]{2,1,0:T(1,128)S(1)} collective-permute-done((f32[4,1,448]{2,1,0:T(1,128)S(1)}, f32[4,1,448]{2,1,0:T(1,128)S(1)}, u32[]{:S(2)}, u32[]{:S(2)}) %collective-permute-start.3) | collective-permute-done | bytes 7200 | tf_op jit(solution)/shard_map/ppermute | solution.py:23
  241.4 0.9 divide_convert_fusion
  242.8 8.3 %fusion.30 = f32[256,7168]{0,1:T(8,128)} fusion(bf16[448,7168]{0,1:T(8,128)(2,1)} %all-gather.10.cloned.1.call-done, bf16[256,896]{1,0:T(8,128)(2,1)S(1)} %bitcast.145, s32[]{:T(128)S(6)} %select_n.115, bf16[256]{0:T(256)(128)(2,1)S(1)} %mul.204), kind=kOutput, calls=%fused_computation.63 | convolution fusion | flops 1644625920 | bytes 14025220 | tf_op jit(solution)/shard_map/dot_general | solution.py:176
  251.1 0.9 copy-done.3
  254.1 16.7 %all_gather.27 = bf16[64,8,2,64]{3,1,2,0:T(8,128)(2,1)S(1)} all-gather(bf16[4,8,2,64]{3,1,2,0:T(8,128)(2,1)S(1)} %copy_select_fusion), channel_id=1, replica_groups=mesh['dp'=16,'mp'=16] {'dp'}, dimensions={0}, use_global_device_ids=true | all-gather | bytes 139264 | tf_op jit(solution)/shard_map/all_gather | solution.py:194
  272.1 71.6 %reduce-scatter.2.cloned.1.call-done = f32[256,448]{0,1:T(8,128)} async-done(((f32[256,7168]{0,1:T(8,128)}), f32[256,448]{0,1:T(8,128)}) %reduce-scatter.2.cloned.1.call-update) | async-done | bytes 458768 | tf_op jit(solution)/shard_map/reduce_scatter | solution.py:181
  343.7 1.1 add_convert_fusion
  344.7 0.8 copy.160
  (165 shorter events, 17.4 us)
Async XLA Ops:
  7.2 132.2 %all-gather.6.cloned.1.call-start = ((), (), s32[]{:S(2)}) async-start(), calls=%async_computation.1 | async-start | bytes 7798784 | tf_op jit(solution)/shard_map/all_gather | solution.py:73
  9.3 101.4 %copy-start.9 = (s32[4,64]{1,0:T(4,128)S(1)}, s32[4,64]{1,0:T(4,128)}, u32[]{:S(2)}) copy-start(s32[4,64]{1,0:T(4,128)} %param.24) | copy-start | bytes 3076
  9.3 151.4 %all-gather.8.cloned.1.call-start = ((), (), s32[]{:S(2)}) async-start(), calls=%async_computation.2 | async-start | bytes 7798784 | tf_op jit(solution)/shard_map/all_gather | solution.py:83
  10.0 232.7 %all-gather.10.cloned.1.call-start = ((), (), s32[]{:S(2)}) async-start(), calls=%async_computation.3 | async-start | bytes 7798784 | tf_op jit(solution)/shard_map/all_gather | solution.py:178
  12.1 331.6 %reduce-scatter.2.cloned.1.call-start = ((), (), s32[]{:S(2)}) async-start(), calls=%async_computation.4 | async-start | bytes 7798784 | tf_op jit(solution)/shard_map/reduce_scatter | solution.py:181
  83.1 29.4 %copy-start.10 = (s32[4]{0:T(128)S(1)}, s32[4]{0:T(128)}, u32[]{:S(2)}) copy-start(s32[4]{0:T(128)} %param.23) | copy-start | bytes 52
  83.1 29.4 %copy-start.6 = (bf16[448,64]{0,1:T(8,128)(2,1)S(1)}, bf16[448,64]{0,1:T(8,128)(2,1)}, u32[]{:S(2)}) copy-start(bf16[448,64]{0,1:T(8,128)(2,1)} %param.19) | copy-start | bytes 172036
  150.7 3.1 copy-start.2
  154.9 2.1 copy-start.1
  156.2 4.0 %collective-permute-start.1 = (bf16[256,64]{0,1:T(8,128)(2,1)S(1)}, bf16[256,64]{0,1:T(8,128)(2,1)S(1)}, u32[]{:S(2)}, u32[]{:S(2)}) collective-permute-start(bf16[256,64]{0,1:T(8,128)(2,1)S(1)} %convolution_convert_fusion.2), channel_id=1, source_target_pairs={{0,1},{1,0},{2,3},{3,2},{4,5},{5,4},{6,7},{7,6},{8,9},{9,8},{10,11... | collective-permute-start | bytes 98312 | tf_op jit(solution)/shard_map/ppermute | solution.py:23
  158.5 10.6 %collective-permute-start.2 = (bf16[256,64]{0,1:T(8,128)(2,1)S(1)}, bf16[256,64]{0,1:T(8,128)(2,1)S(1)}, u32[]{:S(2)}, u32[]{:S(2)}) collective-permute-start(bf16[256,64]{0,1:T(8,128)(2,1)S(1)} %convolution_convert_fusion.1), channel_id=1, source_target_pairs={{0,1},{1,0},{2,3},{3,2},{4,5},{5,4},{6,7},{7,6},{8,9},{9,8},{10,11... | collective-permute-start | bytes 98312 | tf_op jit(solution)/shard_map/ppermute | solution.py:23
  167.8 7.3 %collective-permute-start = (bf16[256,448]{0,1:T(8,128)(2,1)S(1)}, bf16[256,448]{0,1:T(8,128)(2,1)S(1)}, u32[]{:S(2)}, u32[]{:S(2)}) collective-permute-start(bf16[256,448]{0,1:T(8,128)(2,1)S(1)} %convolution_convert_fusion), channel_id=1, source_target_pairs={{0,1},{1,0},{2,3},{3,2},{4,5},{5,4},{6,7},{7,6},{8,9},{9,8},{10,11... | collective-permute-start | bytes 688136 | tf_op jit(solution)/shard_map/ppermute | solution.py:23
  175.9 0.9 copy-start.5
  175.9 1.5 copy-start.4
  176.2 1.1 copy-start.11
  177.4 45.3 %copy-start.8 = (s32[4,64]{1,0:T(4,128)S(1)}, s32[4,64]{1,0:T(4,128)}, u32[]{:S(2)}) copy-start(s32[4,64]{1,0:T(4,128)} %param.25) | copy-start | bytes 3076
  182.6 4.6 %copy-start = (f32[448,2048]{1,0:T(8,128)S(1)}, f32[448,2048]{1,0:T(8,128)}, u32[]{:S(2)}) copy-start(f32[448,2048]{1,0:T(8,128)} %get-tuple-element.351) | copy-start | bytes 11010052 | tf_op jit(solution)/shard_map/while
  183.9 4.1 %copy-start.12 = (s32[4]{0:T(128)S(1)}, s32[4]{0:T(128)}, u32[]{:S(2)}) copy-start(s32[4]{0:T(128)} %get-tuple-element.447) | copy-start | bytes 52 | tf_op jit(solution)/shard_map/while
  193.3 4.5 %copy-start = (f32[448,2048]{1,0:T(8,128)S(1)}, f32[448,2048]{1,0:T(8,128)}, u32[]{:S(2)}) copy-start(f32[448,2048]{1,0:T(8,128)} %get-tuple-element.351) | copy-start | bytes 11010052 | tf_op jit(solution)/shard_map/while
  194.6 4.0 %copy-start.12 = (s32[4]{0:T(128)S(1)}, s32[4]{0:T(128)}, u32[]{:S(2)}) copy-start(s32[4]{0:T(128)} %get-tuple-element.447) | copy-start | bytes 52 | tf_op jit(solution)/shard_map/while
  203.9 4.5 %copy-start = (f32[448,2048]{1,0:T(8,128)S(1)}, f32[448,2048]{1,0:T(8,128)}, u32[]{:S(2)}) copy-start(f32[448,2048]{1,0:T(8,128)} %get-tuple-element.351) | copy-start | bytes 11010052 | tf_op jit(solution)/shard_map/while
  205.2 4.0 %copy-start.12 = (s32[4]{0:T(128)S(1)}, s32[4]{0:T(128)}, u32[]{:S(2)}) copy-start(s32[4]{0:T(128)} %get-tuple-element.447) | copy-start | bytes 52 | tf_op jit(solution)/shard_map/while
  214.4 4.5 %copy-start = (f32[448,2048]{1,0:T(8,128)S(1)}, f32[448,2048]{1,0:T(8,128)}, u32[]{:S(2)}) copy-start(f32[448,2048]{1,0:T(8,128)} %get-tuple-element.351) | copy-start | bytes 11010052 | tf_op jit(solution)/shard_map/while
  215.7 4.0 %copy-start.12 = (s32[4]{0:T(128)S(1)}, s32[4]{0:T(128)}, u32[]{:S(2)}) copy-start(s32[4]{0:T(128)} %get-tuple-element.447) | copy-start | bytes 52 | tf_op jit(solution)/shard_map/while
  219.8 21.7 %collective-permute-start.4 = (f32[4,1,448,128]{3,2,1,0:T(8,128)S(1)}, f32[4,1,448,128]{3,2,1,0:T(8,128)S(1)}, u32[]{:S(2)}, u32[]{:S(2)}) collective-permute-start(f32[4,1,448,128]{3,2,1,0:T(8,128)S(1)} %get-tuple-element.434), channel_id=1, source_target_pairs={{0,1},{1,0},{2,3},{3,2},{4,5},{5,4},{6,7},{7,6},{8,9},{9,8},{10,11... | collective-permute-start | bytes 2752520 | tf_op jit(solution)/shard_map/ppermute | solution.py:23
  220.6 20.7 %collective-permute-start.3 = (f32[4,1,448]{2,1,0:T(1,128)S(1)}, f32[4,1,448]{2,1,0:T(1,128)S(1)}, u32[]{:S(2)}, u32[]{:S(2)}) collective-permute-start(f32[4,1,448]{2,1,0:T(1,128)S(1)} %get-tuple-element.432), channel_id=1, source_target_pairs={{0,1},{1,0},{2,3},{3,2},{4,5},{5,4},{6,7},{7,6},{8,9},{9,8},{10,11... | collective-permute-start | bytes 21512 | tf_op jit(solution)/shard_map/ppermute | solution.py:23
  221.9 19.5 %collective-permute-start.5 = (f32[4,1,448]{2,1,0:T(1,128)S(1)}, f32[4,1,448]{2,1,0:T(1,128)S(1)}, u32[]{:S(2)}, u32[]{:S(2)}) collective-permute-start(f32[4,1,448]{2,1,0:T(1,128)S(1)} %get-tuple-element.433), channel_id=1, source_target_pairs={{0,1},{1,0},{2,3},{3,2},{4,5},{5,4},{6,7},{7,6},{8,9},{9,8},{10,11... | collective-permute-start | bytes 21512 | tf_op jit(solution)/shard_map/ppermute | solution.py:23
  251.1 0.9 copy-start.3
  251.1 1.2 copy-start.7
  251.1 1.3 copy-start.13
Sparse Core Ops, SparseCore 0:
  10.5 74.5 all-gather.5
  86.9 57.1 all-gather.7
  146.0 50.0 all-gather.9
  251.2 92.3 reduce-scatter.1
where the time goes:
time: 353 us; the launch traced here: 352 us
  blocking collectives  134 us (38%)
  waiting for transfers between devices  96.3 us (27%)
  matrix products  51.8 us (15%)
  local copies, waits for them, and re-layouts  31.2 us (9%)
  between operations  15 us (4%)
  other arithmetic  14.3 us (4%)
  starting transfers between devices  6.29 us (2%)
    reduce_scatter x1, waiting for transfers between devices, shards(): mine = lax.psum_scatter(terms, 'mp', scatter_dimension=1, tiled=True)  71.6 us
    unnamed x1, blocking collectives  68 us
    all_gather x1, blocking collectives, shards(): lax.all_gather(w_key, 'dp', axis=0, tiled=True)  25.8 us
    ppermute x6, waiting for transfers between devices, from_partner(): return lax.ppermute(block, axis, route)  23.9 us
    all_gather x1, blocking collectives, shards(): lax.all_gather(w_value, 'dp', axis=0, tiled=True)  23.8 us
    all_gather x1, blocking collectives, shards(): every_row = lax.all_gather(chosen, 'dp', axis=0, tiled=True)  16.7 us
    dot_general x4, matrix products, one_request(): jnp.einsum('gqd,gkd->gqk', queries, cached_keys, preferred_element_type=j...  14.5 us
    dot_general x4, matrix products, one_request(): jnp.einsum('gqk,gkd->gqd', probs_cache, cached_values, preferred_element_...  12.4 us
  transfers between devices with their start and end apart: 10, of which 4 were waited for; matrix products, arithmetic and copies ran while one was open for 24% of the time, Pallas kernels for 0%

commit v1 on v0

v1 whole, which is shorter than its diff:
```python
import functools
import math

import jax
import jax.numpy as jnp
from jax import lax
from jax.experimental import pallas as pl
from jax.experimental.pallas import tpu as pltpu
from jax.sharding import PartitionSpec as P

GROUP = 7
SIDE = 4
epsilon = 1e-05
rope_base = 5000000.0
masked_score = -1e30
bf16 = jnp.bfloat16
f32 = jnp.float32
VMEM = pltpu.VMEM


def whole():
    return pl.BlockSpec(memory_space=VMEM)


def scalars():
    return pl.BlockSpec(memory_space=pltpu.SMEM)


def params(mib):
    return pltpu.CompilerParams(vmem_limit_bytes=mib * 2**20)


def shift_dp(block, step):
    return lax.ppermute(block, "dp", [(i, (i + step) % 16) for i in range(16)])


def other_core(block):
    return lax.ppermute(block, "dp", [(i, i ^ 1) for i in range(16)])


def shift_y(block, step):
    return lax.ppermute(block, "mp", [(i, i // 4 * 4 + (i + step) % 4) for i in range(16)])


def shift_x(block, step):
    return lax.ppermute(block, "mp", [(i, (i + 4 * step) % 16) for i in range(16)])


def partner(block):
    return lax.ppermute(block, "mp", [(i, i ^ 1) for i in range(16)])


def tree_closure(parents):
    width = parents.shape[-1]
    nodes = jnp.arange(width, dtype=jnp.int32)
    onehot = (parents[..., None] == nodes).astype(f32)
    reach = jnp.minimum(jnp.eye(width, dtype=f32) + onehot, 1.0)
    for _ in range((width - 1).bit_length()):
        small = reach.astype(bf16)
        reach = jnp.minimum(
            jnp.einsum("rij,rjk->rik", small, small, preferred_element_type=f32), 1.0
        )
    return reach


def project_kernel(order, x_ref, *refs):
    full, halves = refs[:14], refs[14:18]
    out_ref, total, inv_ref, joined = refs[18:]
    rows = out_ref.shape[0]
    half_rows = halves[0].shape[0]
    for c in range(2):
        joined[c, :half_rows] = halves[2 * c][...]
        joined[c, half_rows:] = halves[2 * c + 1][...]
    width = x_ref.shape[0] * x_ref.shape[2]

    @pl.loop(0, rows // 32)
    def _(chunk):
        at = pl.ds(pl.multiple_of(chunk * 32, 32), 32)
        squares = jnp.zeros((32, x_ref.shape[2]), f32)
        for b in range(x_ref.shape[0]):
            part = x_ref[b, at, :].astype(f32)
            squares = squares + part * part
        mean = jnp.sum(squares, -1, keepdims=True) / width
        inv_ref[at, :] = jnp.broadcast_to(lax.rsqrt(mean + epsilon), (32, 128))

    inverse = inv_ref[:, :1]
    for slot in range(16):
        block = order[slot]
        gain = x_ref[block, rows : rows + 16, :][:1].astype(f32)
        normed = (x_ref[block, :rows, :].astype(f32) * inverse * gain).astype(bf16)
        weight = full[slot][...] if slot < 14 else joined[slot - 14]
        term = jnp.dot(normed, weight, preferred_element_type=f32)
        if slot == 0:
            total[...] = term
        else:
            total[...] += term
    out_ref[...] = total[...].astype(bf16)


def project(order, gathered, blocks):
    rows = gathered.shape[1] - 16
    columns = blocks[0].shape[1]
    return pl.pallas_call(
        project_kernel,
        out_shape=jax.ShapeDtypeStruct((rows, columns), bf16),
        in_specs=[scalars()] + [whole()] * 19,
        out_specs=whole(),
        scratch_shapes=[
            pltpu.VMEM((rows, columns), f32),
            pltpu.VMEM((rows, 128), f32),
            pltpu.VMEM((2,) + blocks[0].shape, bf16),
        ],
        compiler_params=params(40),
        name="project",
    )(order, gathered, *blocks)


def attention_kernel(
    facts, own_ref, oth_ref, cos_ref, sin_ref, reach_ref, pick_ref, key_ref, value_ref,
    kept_ref, sent_ref, stats_ref, chosen_ref, scores, top,
):
    request = pl.program_id(0)
    first = facts[0] == 0
    count = facts[1 + request]
    nodes = own_ref.shape[0]
    q_cols = 448
    cosine, sine = cos_ref[...], sin_ref[...]
    own, other = own_ref[...].astype(f32), oth_ref[...].astype(f32)

    def paired(lo, hi):
        low = jnp.where(first, own[:, lo:hi], other[:, lo:hi])
        high = jnp.where(first, other[:, lo:hi], own[:, lo:hi])
        return jnp.concatenate([low, high], 1)

    def turned(u):
        return (u * cosine + pltpu.roll(u, 64, 1) * sine).astype(bf16)

    query = paired(0, q_cols)
    queries = jnp.concatenate(
        [turned(query[:, 128 * g : 128 * g + 128]) for g in range(GROUP)], 0
    )
    rot_key = turned(paired(q_cols, q_cols + 64))
    node_value = paired(q_cols + 64, q_cols + 128).astype(bf16)

    wide = rot_key.astype(f32)
    own_key = jnp.where(first, wide[:, :64], wide[:, 64:])
    kv_rows = jnp.concatenate([own_key, own[:, q_cols + 64 : q_cols + 128]], 1).astype(bf16)
    chosen_ref[0] = jnp.dot(pick_ref[0], kv_rows, preferred_element_type=f32).astype(bf16)

    span = scores.shape[2]
    rows = GROUP * nodes
    tree = lax.dot_general(queries, rot_key, (((1,), (1,)), ((), ())), preferred_element_type=f32)
    reach = jnp.concatenate([reach_ref[0]] * GROUP, 0)
    tree = jnp.where(jnp.logical_and(reach > 0.5, first), tree, masked_score)
    top[...] = jnp.broadcast_to(jnp.max(tree, -1, keepdims=True), top.shape)
    pieces = scores.shape[0]
    for c in range(pieces):

        @pl.when(count > c * span)
        def _(c=c):
            part = lax.dot_general(
                queries, key_ref[0, c * span : (c + 1) * span, :],
                (((1,), (1,)), ((), ())), preferred_element_type=f32,
            )
            live = lax.broadcasted_iota(jnp.int32, (1, span), 1) + c * span < count
            part = jnp.where(live, part, masked_score)
            scores[c] = part
            top[...] = jnp.maximum(top[...], jnp.max(part, -1, keepdims=True))

    highest = top[:, :1]
    factor = math.log2(math.e) / math.sqrt(128.0)
    ones = jnp.ones((span, 128), bf16)
    weights = jnp.where(
        jnp.logical_and(reach > 0.5, first), jnp.exp2((tree - highest) * factor), 0.0
    ).astype(bf16)
    summed = jnp.dot(
        weights, jnp.concatenate([node_value, ones[:nodes]], 1), preferred_element_type=f32
    )

    def add(c, carried):
        weights = jnp.exp2((scores[c] - highest) * factor).astype(bf16)
        at = pl.ds(pl.multiple_of(c * span, span), span)
        return carried + jnp.dot(
            weights,
            jnp.concatenate([value_ref[0, at, :], ones], 1),
            preferred_element_type=f32,
        )

    summed = lax.fori_loop(0, (count + span - 1) // span, add, summed)
    total = summed[:, 128:129]
    some = total > 0.0
    safe = jnp.where(some, total, 1.0)
    mean = summed[:, :128] / safe
    level = jnp.where(some, highest * (1.0 / math.sqrt(128.0)) + jnp.log(safe), masked_score)
    every = jnp.concatenate([mean[g * nodes : (g + 1) * nodes] for g in range(GROUP)], 1)
    low, high = every[:, :q_cols], every[:, q_cols:]
    kept_ref[...] = jnp.where(first, low, high)
    levels = jnp.concatenate(
        [level[g * nodes : (g + 1) * nodes] for g in range(GROUP)]
        + [jnp.zeros((nodes, 128 - GROUP), f32)], 1,
    )
    stats_ref[...] = levels
    coarse = levels[:, :16].astype(bf16).astype(f32)
    finer = (levels[:, :16] - coarse).astype(bf16).astype(f32)
    finest = levels[:, :16] - coarse - finer
    sent_ref[...] = jnp.concatenate(
        [jnp.where(first, high, low), coarse, finer, finest, jnp.zeros((nodes, 16), f32)], 1
    ).astype(bf16)


def attention(facts, own, other, cosine, sine, reach, pick, keys, values):
    requests, half_len, head = keys.shape
    nodes = own.shape[0] // requests
    columns = own.shape[1]

    def rows_of(width):
        return pl.BlockSpec((nodes, width), lambda r, facts: (r, 0))

    def request_of(*shape):
        return pl.BlockSpec((1,) + shape, lambda r, facts: (r, 0, 0))

    span = 512
    return pl.pallas_call(
        attention_kernel,
        grid_spec=pltpu.PrefetchScalarGridSpec(
            num_scalar_prefetch=1,
            grid=(requests,),
            in_specs=[
                rows_of(columns), rows_of(columns), rows_of(head), rows_of(head),
                request_of(nodes, nodes), request_of(*pick.shape[1:]),
                request_of(half_len, head), request_of(half_len, head),
            ],
            out_specs=[rows_of(448), rows_of(512), rows_of(128), request_of(pick.shape[1], 128)],
            scratch_shapes=[
                pltpu.VMEM((half_len // span, GROUP * nodes, span), f32),
                pltpu.VMEM((GROUP * nodes, 128), f32),
            ],
        ),
        out_shape=[
            jax.ShapeDtypeStruct((requests * nodes, 448), f32),
            jax.ShapeDtypeStruct((requests * nodes, 512), bf16),
            jax.ShapeDtypeStruct((requests * nodes, 128), f32),
            jax.ShapeDtypeStruct((requests, pick.shape[1], 128), bf16),
        ],
        compiler_params=params(28),
        name="attention",
    )(facts, own, other, cosine, sine, reach, pick, keys, values)


def combine_kernel(facts, kept_ref, stats_ref, got_ref, valid_ref, out_ref):
    first = facts[0] == 0
    got = got_ref[...].astype(f32)
    theirs = got[:, 448:464] + got[:, 464:480] + got[:, 480:496]
    ours = stats_ref[:, :16]
    highest = jnp.maximum(ours, theirs)
    own_factor = jnp.exp(ours - highest)
    other_factor = jnp.exp(theirs - highest)
    both = own_factor + other_factor

    def spread(part):
        rows = part.shape[0]
        every = jnp.concatenate(
            [jnp.broadcast_to(part[:, g : g + 1], (rows, 128)) for g in range(GROUP)], 1
        )
        return jnp.where(first, every[:, :448], every[:, 448:])

    mixed = kept_ref[...] * spread(own_factor / both) + got[:, :448] * spread(other_factor / both)
    out_ref[...] = mixed.astype(bf16) * valid_ref[...]


def combine(facts, kept, stats, got, valid):
    return pl.pallas_call(
        combine_kernel,
        out_shape=jax.ShapeDtypeStruct(kept.shape, bf16),
        in_specs=[scalars()] + [whole()] * 4,
        out_specs=whole(),
        compiler_params=params(16),
        name="combine",
    )(facts, kept, stats, got, valid)


def out_kernel(steps, place, att_ref, weight_ref, *outs):
    half = att_ref.shape[0] // 2
    x, y = place[0], place[1]
    for k, step in enumerate(steps):
        for along in range(SIDE):
            block = along * SIDE + lax.rem(y + step, SIDE)
            outs[2 * k][along] = jnp.dot(
                att_ref[:half, :], weight_ref[block], preferred_element_type=f32
            ).astype(outs[2 * k].dtype)
        for along in range(SIDE):
            block = lax.rem(x + step, SIDE) * SIDE + along
            outs[2 * k + 1][along] = jnp.dot(
                att_ref[half:, :], weight_ref[block], preferred_element_type=f32
            ).astype(outs[2 * k + 1].dtype)


def out_terms(steps, place, att, weights):
    half, columns = att.shape[0] // 2, weights.shape[2]
    return pl.pallas_call(
        functools.partial(out_kernel, steps),
        out_shape=[
            jax.ShapeDtypeStruct((SIDE, half, columns), bf16 if step else f32)
            for step in steps
            for _ in range(2)
        ],
        in_specs=[scalars(), whole(), whole()],
        out_specs=[whole()] * (2 * len(steps)),
        compiler_params=params(24),
        name="out_terms",
    )(place, att, weights)


def partial_kernel(place, own_ref, *refs):
    got, outs = refs[:3], refs[3:]
    for step in range(SIDE):
        at = lax.rem(place[0] + step, SIDE)
        value = own_ref[at]
        for part in got:
            value = value + part[at].astype(f32)
        outs[step][...] = value.astype(outs[step].dtype)


def partial_sums(place, own, got):
    shape = own.shape[1:]
    return pl.pallas_call(
        partial_kernel,
        out_shape=[jax.ShapeDtypeStruct(shape, bf16 if step else f32) for step in range(SIDE)],
        in_specs=[scalars()] + [whole()] * 4,
        out_specs=[whole()] * SIDE,
        compiler_params=params(16),
        name="partial_sums",
    )(place, own, *got)


def final_kernel(hidden_ref, *refs):
    out_ref = refs[-1]
    half = hidden_ref.shape[0] // 2
    for h in range(2):
        own, *got = refs[4 * h : 4 * h + 4]
        value = own[...]
        for part in got:
            value = value + part[...].astype(f32)
        at = slice(h * half, (h + 1) * half)
        out_ref[at] = (hidden_ref[at].astype(f32) + value).astype(bf16)


def final(hidden, parts):
    return pl.pallas_call(
        final_kernel,
        out_shape=jax.ShapeDtypeStruct(hidden.shape, bf16),
        in_specs=[whole()] * 9,
        out_specs=whole(),
        compiler_params=params(16),
        name="final",
    )(hidden, *parts)


def shards(
    hidden_in,
    norm_gain,
    w_query,
    w_key,
    w_value,
    w_out,
    key_cache,
    value_cache,
    cache_len,
    tree_parent,
    valid_nodes,
    accepted_path,
    slot_owner,
):
    req_dev, tree_size, part_width = hidden_in.shape
    row_count = req_dev * tree_size
    head_dim = key_cache.shape[-1]
    half_len = key_cache.shape[3]
    dp, mp = lax.axis_index("dp"), lax.axis_index("mp")
    half_index = mp % 2
    hidden = hidden_in.reshape(row_count, part_width)

    weights = jnp.concatenate([w_query, w_key, w_value], 1)
    packed = jnp.concatenate([hidden, jnp.broadcast_to(norm_gain[None], (16, part_width))], 0)
    gathered = lax.all_gather(packed, "mp")

    full, order = [weights, other_core(weights)], [dp, dp ^ 1]
    up = down = weights
    for step in range(1, 4):
        up, down = shift_dp(up, 2), shift_dp(down, -2)
        full += [up, down, other_core(up), other_core(down)]
        order += [dp - 2 * step, dp + 2 * step, (dp ^ 1) - 2 * step, (dp ^ 1) + 2 * step]
    cut = weights.shape[0] // 2
    up, down = shift_dp(up[:cut], 2), shift_dp(down[cut:], -2)
    halves = [up, down, other_core(up), other_core(down)]
    order += [dp + 8, (dp ^ 1) + 8]
    order = (jnp.stack(order) % 16).astype(jnp.int32)

    reach = tree_closure(tree_parent)
    depth = jnp.sum(reach, -1) - 1.0
    position = (cache_len[:, None].astype(f32) + depth).reshape(row_count, 1)
    half_dim = head_dim // 2
    inverse = jnp.exp(
        jnp.arange(half_dim, dtype=f32) * (-2.0 * math.log(rope_base) / head_dim)
    )
    angles = position * inverse
    cosine, sine = jnp.cos(angles), jnp.sin(angles)
    cosine = jnp.concatenate([cosine, cosine], -1)
    sine = jnp.concatenate([-sine, sine], -1)
    pick = (
        jnp.pad(accepted_path, ((0, 0), (0, 8)))[..., None]
        == jnp.arange(tree_size, dtype=jnp.int32)
    ).astype(bf16)
    counts = jnp.clip(cache_len - half_index * half_len, 0, half_len)
    facts = jnp.concatenate([half_index[None], counts]).astype(jnp.int32)
    valid = valid_nodes.reshape(row_count, 1).astype(bf16)
    place = jnp.stack([mp // SIDE, mp % SIDE]).astype(jnp.int32)

    own = project(order, gathered, full + halves)
    other = partner(own)

    w_out_late, _ = lax.optimization_barrier((w_out, gathered[0, 0, 0]))
    w_out_all = lax.all_gather(w_out_late, "dp")

    kept, sent, stats, chosen = attention(
        facts, own, other, cosine, sine, reach, pick, key_cache[:, 0, 0], value_cache[:, 0, 0]
    )
    attended = combine(facts, kept, stats, partner(sent), valid)

    a2, b2, a1, b1 = out_terms((2, 1), place, attended, w_out_all)
    a3, b3, a0, b0 = out_terms((3, 0), place, attended, w_out_all)
    got_a = [shift_y(a2, 2), shift_y(a1, 1), shift_y(a3, 3)]
    got_b = [shift_x(b2, 2), shift_x(b1, 1), shift_x(b3, 3)]
    a = partial_sums(place[:1], a0, got_a)
    b = partial_sums(place[1:], b0, got_b)
    parts = [a[0]] + [shift_x(a[s], s) for s in (2, 1, 3)]
    parts += [b[0]] + [shift_y(b[s], s) for s in (2, 1, 3)]
    layer_out = final(hidden, parts).reshape(req_dev, tree_size, part_width)

    every_row = lax.all_gather(chosen[:, : accepted_path.shape[1]], "dp", axis=0, tiled=True)
    total_reqs = slot_owner.shape[0]
    my_slots = dp * req_dev + jnp.arange(req_dev, dtype=jnp.int32)
    senders = (slot_owner[None, :] == my_slots[:, None]).astype(bf16)
    accepted_kv = (
        jnp.dot(senders, every_row.reshape(total_reqs, -1), preferred_element_type=f32)
        .astype(bf16)
        .reshape(req_dev, accepted_path.shape[1], 2, -1)
    )
    return (layer_out, accepted_kv)


def solution(mesh):
    placed = (
        P("dp", None, "mp"),
        P("mp"),
        P("dp", "mp"),
        P("dp", "mp"),
        P("dp", "mp"),
        P("mp", "dp"),
        P("dp", "mp", None, None, None),
        P("dp", "mp", None, None, None),
        P("dp"),
        P("dp", None),
        P("dp", None),
        P("dp", None),
        P(),
    )
    return jax.shard_map(
        shards,
        mesh=mesh,
        in_specs=placed,
        out_specs=(P("dp", None, "mp"), P("dp", None, None, "mp")),
        check_vma=False,
    )
```

time: 353 us -> 208 us (0.59)
  blocking collectives: 134 us -> 15.8 us
  matrix products: 51.8 us -> 1.89 us
  Pallas kernels: 0 us -> 35.7 us
  starting transfers between devices: 6.29 us -> 38.5 us
  local copies, waits for them, and re-layouts: 31.2 us -> 11.5 us
  waiting for transfers between devices: 96.3 us -> 83.5 us
  other arithmetic: 14.3 us -> 3.57 us
    reduce_scatter x1 -> x0, waiting for transfers between devices: 71.6 us -> none  [shards(): mine = lax.psum_scatter(terms, 'mp', scatter_dimension=1, tiled=True)]
    unnamed x1 -> x0, blocking collectives: 68 us -> none
    ppermute x6 -> x31, waiting for transfers between devices: 23.9 us -> 78.3 us  [the longest x8 40 us: shift_dp(): return lax.ppermute(block, 'dp', [(i, (i + step) % 16) for i in range(16)])]
    all_gather x3 -> x1, blocking collectives: 66.2 us -> 15.8 us  [shards(): lax.all_gather(chosen[:, :accepted_path.shape[1]], 'dp', axis=0, tiled=True)]
    dot_general x26 -> x4, matrix products: 51.8 us -> 1.89 us  [the longest x3 1.7 us: tree_closure(): jnp.einsum('rij,rjk->rik', small, small, preferred_element_type=f32)]
    pallas_call x0 -> x8, Pallas kernels: none -> 35.7 us  [the longest x1 16.5 us: attention(): pl.pallas_call(attention_kernel, grid_spec=pltpu.PrefetchScalarGridSpec(n...]
    ppermute x6 -> x31, starting transfers between devices: 6.13 us -> 38.4 us  [the longest x8 16.5 us: shift_dp(): return lax.ppermute(block, 'dp', [(i, (i + step) % 16) for i in range(16)])]
    all_gather x3 -> x0, local copies, waits for them, and re-layouts: 12.5 us -> none  [the longest x1 11.3 us: shards(): lax.all_gather(hidden_in, 'mp', axis=2, tiled=True)]
  transfers between devices with their start and end apart: 10 -> 33, of which waited for: 4 -> 16; matrix products, arithmetic and copies ran while one was open for 24% -> 3% of each run, Pallas kernels for 0% -> 16%
where the time goes in v1:
time: 208 us; the launch traced here: 205 us
  waiting for transfers between devices  83.5 us (40%)
  starting transfers between devices  38.5 us (19%)
  Pallas kernels  35.7 us (17%)
  blocking collectives  15.8 us (8%)
  between operations  14.4 us (7%)
  local copies, waits for them, and re-layouts  11.5 us (6%)
  other arithmetic  3.57 us (2%)
    ppermute x8, waiting for transfers between devices, shift_dp(): return lax.ppermute(block, 'dp', [(i, (i + step) % 16) for i in range(16)])  40 us
    ppermute x6, waiting for transfers between devices, shift_x(): lax.ppermute(block, 'mp', [(i, (i + 4 * step) % 16) for i in range(16)])  23.3 us
    pallas_call x1, Pallas kernels, attention(): pl.pallas_call(attention_kernel, grid_spec=pltpu.PrefetchScalarGridSpec(n...  16.5 us
    ppermute x8, starting transfers between devices, shift_dp(): return lax.ppermute(block, 'dp', [(i, (i + step) % 16) for i in range(16)])  16.5 us
    all_gather x1, blocking collectives, shards(): lax.all_gather(chosen[:, :accepted_path.shape[1]], 'dp', axis=0, tiled=True)  15.8 us
    ppermute x2, waiting for transfers between devices, partner(): return lax.ppermute(block, 'mp', [(i, i ^ 1) for i in range(16)])  14.1 us
    ppermute x6, starting transfers between devices, shift_y(): lax.ppermute(block, 'mp', [(i, i // 4 * 4 + (i + step) % 4) for i in rang...  11.3 us
    unnamed x42, local copies, waits for them, and re-layouts  8.23 us
  transfers between devices with their start and end apart: 33, of which 16 were waited for; matrix products, arithmetic and copies ran while one was open for 3% of the time, Pallas kernels for 16%

profile of v1, /device:TPU:6, one launch (start us, length us, event | category | flops | bytes accessed | tf_op | source)
XLA Modules:
  0.0 204.8 jit_solution(5190690544956663385)
XLA Ops:
  7.2 0.7 broadcast_in_dim.5
  8.0 1.7 pad_maximum_fusion.1
  10.9 2.0 collective-permute-start.1
  12.9 4.0 %collective-permute-start.2 = (bf16[448,576]{1,0:T(8,128)(2,1)S(1)}, bf16[448,576]{1,0:T(8,128)(2,1)S(1)}, u32[]{:S(2)}, u32[]{:S(2)}) collective-permute-start(bf16[448,576]{1,0:T(8,128)(2,1)S(1)} %pad_maximum_fusion.refs_0_), channel_id=1, source_target_pairs={{0,224},{16,240},{32,0},{48,16},{64,32},{80,48},{96,64},{112,80},{... | collective-permute-start | bytes 1548296 | tf_op jit(solution)/shard_map/ppermute | solution.py:34
  16.9 12.9 %collective-permute-done.1.refs_2_ = bf16[448,576]{1,0:T(8,128)(2,1)S(1)} collective-permute-done((bf16[448,576]{1,0:T(8,128)(2,1)S(1)}, bf16[448,576]{1,0:T(8,128)(2,1)S(1)}, u32[]{:S(2)}, u32[]{:S(2)}) %collective-permute-start.1) | collective-permute-done | bytes 516128 | tf_op jit(solution)/shard_map/ppermute | solution.py:34
  29.8 3.2 %collective-permute-start.6 = (bf16[448,576]{1,0:T(8,128)(2,1)S(1)}, bf16[448,576]{1,0:T(8,128)(2,1)}, u32[]{:S(2)}, u32[]{:S(2)}) collective-permute-start(bf16[448,576]{1,0:T(8,128)(2,1)S(1)} %collective-permute-done.2.refs_3_), channel_id=1, source_target_pairs={{0,224},{16,240},{32,0},{48,16},{64,32},{80,48},{96,64},{112,80},{... | collective-permute-start | bytes 1548296 | tf_op jit(solution)/shard_map/ppermute | solution.py:34
  33.1 12.2 %collective-permute-done.5.refs_6_ = bf16[448,576]{1,0:T(8,128)(2,1)S(1)} collective-permute-done((bf16[448,576]{1,0:T(8,128)(2,1)S(1)}, bf16[448,576]{1,0:T(8,128)(2,1)S(1)}, u32[]{:S(2)}, u32[]{:S(2)}) %collective-permute-start.5) | collective-permute-done | bytes 516128 | tf_op jit(solution)/shard_map/ppermute | solution.py:34
  46.1 3.7 %collective-permute-start.10 = (bf16[448,576]{1,0:T(8,128)(2,1)}, bf16[448,576]{1,0:T(8,128)(2,1)S(1)}, u32[]{:S(2)}, u32[]{:S(2)}) collective-permute-start(bf16[448,576]{1,0:T(8,128)(2,1)} %collective-permute-done.6.refs_7_), channel_id=1, source_target_pairs={{0,224},{16,240},{32,0},{48,16},{64,32},{80,48},{96,64},{112,80},{... | collective-permute-start | bytes 1548296 | tf_op jit(solution)/shard_map/ppermute | solution.py:34
  49.8 1.0 fusion.27
  51.2 8.6 %collective-permute-done.9.refs_10_ = bf16[448,576]{1,0:T(8,128)(2,1)S(1)} collective-permute-done((bf16[448,576]{1,0:T(8,128)(2,1)S(1)}, bf16[448,576]{1,0:T(8,128)(2,1)S(1)}, u32[]{:S(2)}, u32[]{:S(2)}) %collective-permute-start.9) | collective-permute-done | bytes 516128 | tf_op jit(solution)/shard_map/ppermute | solution.py:34
  60.0 0.8 slice.13
  60.7 1.5 collective-permute-done.10.refs_11_
  62.8 0.7 slice.14
  63.6 3.0 %collective-permute-start.14 = (bf16[224,576]{1,0:T(8,128)(2,1)}, bf16[224,576]{1,0:T(8,128)(2,1)}, u32[]{:S(2)}, u32[]{:S(2)}) collective-permute-start(bf16[224,576]{1,0:T(8,128)(2,1)} %slice.14), channel_id=1, source_target_pairs={{0,224},{16,240},{32,0},{48,16},{64,32},{80,48},{96,64},{112,80},{... | collective-permute-start | bytes 774152 | tf_op jit(solution)/shard_map/ppermute | solution.py:34
  67.8 4.2 %collective-permute-done.13.refs_14_ = bf16[224,576]{1,0:T(8,128)(2,1)} collective-permute-done((bf16[224,576]{1,0:T(8,128)(2,1)}, bf16[224,576]{1,0:T(8,128)(2,1)}, u32[]{:S(2)}, u32[]{:S(2)}) %collective-permute-start.13) | collective-permute-done | bytes 258080 | tf_op jit(solution)/shard_map/ppermute | solution.py:34
  72.6 0.9 pad_maximum_fusion.2
  74.6 2.3 %copy-done.1 = bf16[4352,448]{1,0:T(8,128)(2,1)S(1)} copy-done((bf16[4352,448]{1,0:T(8,128)(2,1)S(1)}, bf16[4352,448]{1,0:T(8,128)(2,1)}, u32[]{:S(2)}) %copy-start.1) | copy-done | bytes 3899416
  76.9 7.7 %project.1.own_ref = bf16[256,576]{1,0:T(8,128)(2,1)S(1)} custom-call(s32[16]{0:T(128)S(1)} %and_select_fusion.order, bf16[16,272,448]{2,1,0:T(8,128)(2,1)S(1)} %bitcast.35, bf16[448,576]{1,0:T(8,128)(2,1)S(1)} %pad_maximum_fusion.refs_0_, bf16[448,576]{1,0:T(8,128)(2,1)} %collective-permute-done.refs_1_, ...), custom_call_target="tpu_custom_call" | custom-call | tf_op jit(solution)/shard_map/project/pallas_call | solution.py:103
  84.6 1.7 collective-permute-start.17
  86.4 8.0 %collective-permute-done.17.oth_ref = bf16[256,576]{1,0:T(8,128)(2,1)S(1)} collective-permute-done((bf16[256,576]{1,0:T(8,128)(2,1)S(1)}, bf16[256,576]{1,0:T(8,128)(2,1)S(1)}, u32[]{:S(2)}, u32[]{:S(2)}) %collective-permute-start.17) | collective-permute-done | bytes 294944 | tf_op jit(solution)/shard_map/ppermute | solution.py:50
  94.5 16.5 %attention.1 = (f32[256,448]{1,0:T(8,128)S(1)}, bf16[256,512]{1,0:T(8,128)(2,1)S(1)}, f32[256,128]{1,0:T(8,128)S(1)}, bf16[4,16,128]{2,1,0:T(8,128)(2,1)S(1)}) custom-call(s32[5]{0:T(128)S(1)} %pad_add_fusion.1.facts, bf16[256,576]{1,0:T(8,128)(2,1)S(1)} %project.1.own_ref, bf16[256,576]{1,0:T(8,128)(2,1)S(1)} %collective-permute-done.17.oth_ref, ...), custom_call_target="tpu_custom_call" | custom-call | tf_op jit(solution)/shard_map/attention/pallas_call | solution.py:223
  111.4 6.1 %collective-permute-done.18.got_ref = bf16[256,512]{1,0:T(8,128)(2,1)S(1)} collective-permute-done((bf16[256,512]{1,0:T(8,128)(2,1)S(1)}, bf16[256,512]{1,0:T(8,128)(2,1)S(1)}, u32[]{:S(2)}, u32[]{:S(2)}) %collective-permute-start.18) | collective-permute-done | bytes 262176 | tf_op jit(solution)/shard_map/ppermute | solution.py:50
  117.5 1.9 combine.1.att_ref
  119.4 4.5 %all-gather.7.cloned.1.call-done = bf16[7168,448]{1,0:T(8,128)(2,1)} async-done(((bf16[448,448]{1,0:T(8,128)(2,1)}), bf16[7168,448]{1,0:T(8,128)(2,1)}) %all-gather.7.cloned.1.call-update) | async-done | bytes 6422544 | tf_op jit(solution)/shard_map/all_gather | solution.py:422
  123.9 3.1 %copy-done = bf16[7168,448]{1,0:T(8,128)(2,1)S(1)} copy-done((bf16[7168,448]{1,0:T(8,128)(2,1)S(1)}, bf16[7168,448]{1,0:T(8,128)(2,1)}, u32[]{:S(2)}) %copy-start) | copy-done | bytes 6422552
  127.0 1.8 out_terms.2
  128.8 0.9 collective-permute-start.27
  129.7 2.9 %out_terms.3 = (bf16[4,128,448]{2,1,0:T(8,128)(2,1)}, bf16[4,128,448]{2,1,0:T(8,128)(2,1)}, bf16[4,128,448]{2,1,0:T(8,128)(2,1)}, bf16[4,128,448]{2,1,0:T(8,128)(2,1)}) custom-call(s32[2]{0:T(128)S(1)} %pad_add_fusion.place, bf16[256,448]{1,0:T(8,128)(2,1)S(1)} %combine.1.att_ref, bf16[16,448,448]{2,1,0:T(8,128)(2,1)S(1)} %bitcast.34), custom_call_target="tpu_custom_call" | custom-call | tf_op jit(solution)/shard_map/out_terms/pallas_call | solution.py:300
  132.6 1.2 collective-permute-start.25
  133.7 2.1 %collective-permute-start.26 = (bf16[4,128,448]{2,1,0:T(8,128)(2,1)}, bf16[4,128,448]{2,1,0:T(8,128)(2,1)}, u32[]{:S(2)}, u32[]{:S(2)}) collective-permute-start(bf16[4,128,448]{2,1,0:T(8,128)(2,1)} %get-tuple-element.35), channel_id=1, source_target_pairs={{0,4},{1,5},{2,6},{3,7},{4,8},{5,9},{6,10},{7,11},{8,12},{9,13},{1... | collective-permute-start | bytes 1376264 | tf_op jit(solution)/shard_map/ppermute | solution.py:46
  135.8 2.7 %collective-permute-start.21 = (bf16[4,128,448]{2,1,0:T(8,128)(2,1)}, bf16[4,128,448]{2,1,0:T(8,128)(2,1)S(1)}, u32[]{:S(2)}, u32[]{:S(2)}) collective-permute-start(bf16[4,128,448]{2,1,0:T(8,128)(2,1)} %get-tuple-element.28), channel_id=1, source_target_pairs={{0,3},{1,0},{2,1},{3,2},{4,7},{5,4},{6,5},{7,6},{8,11},{9,8},{10,9... | collective-permute-start | bytes 1376264 | tf_op jit(solution)/shard_map/ppermute | solution.py:42
  138.6 0.8 collective-permute-start.19
  139.4 16.0 %collective-permute-done.27.refs_2_ = bf16[4,128,448]{2,1,0:T(8,128)(2,1)S(1)} collective-permute-done((bf16[4,128,448]{2,1,0:T(8,128)(2,1)S(1)}, bf16[4,128,448]{2,1,0:T(8,128)(2,1)S(1)}, u32[]{:S(2)}, u32[]{:S(2)}) %collective-permute-start.27) | collective-permute-done | bytes 458784 | tf_op jit(solution)/shard_map/ppermute | solution.py:46
  155.4 0.8 copy-done.8
  156.2 1.5 collective-permute-start.20
  157.7 1.5 collective-permute-done.26.refs_1_
  159.2 1.0 copy-done.9
  160.3 2.0 partial_sums.3
  162.3 0.7 copy-done.10
  163.0 3.0 %collective-permute-start.28 = (bf16[128,448]{1,0:T(8,128)(2,1)S(1)}, bf16[128,448]{1,0:T(8,128)(2,1)S(1)}, u32[]{:S(2)}, u32[]{:S(2)}) collective-permute-start(bf16[128,448]{1,0:T(8,128)(2,1)S(1)} %get-tuple-element.38), channel_id=1, source_target_pairs={{0,2},{1,3},{2,0},{3,1},{4,6},{5,7},{6,4},{7,5},{8,10},{9,11},{10,... | collective-permute-start | bytes 344072 | tf_op jit(solution)/shard_map/ppermute | solution.py:42
  166.0 15.8 %all_gather.19 = bf16[64,8,128]{2,1,0:T(8,128)(2,1)S(1)} all-gather(bf16[4,8,128]{2,1,0:T(8,128)(2,1)S(1)} %slice.12), channel_id=1, replica_groups=mesh['dp'=16,'mp'=16] {'dp'}, dimensions={0}, use_global_device_ids=true | all-gather | bytes 139264 | tf_op jit(solution)/shard_map/all_gather | solution.py:439
  182.4 2.7 %collective-permute-start.30 = (bf16[128,448]{1,0:T(8,128)(2,1)S(1)}, bf16[128,448]{1,0:T(8,128)(2,1)S(1)}, u32[]{:S(2)}, u32[]{:S(2)}) collective-permute-start(bf16[128,448]{1,0:T(8,128)(2,1)S(1)} %get-tuple-element.40), channel_id=1, source_target_pairs={{0,3},{1,0},{2,1},{3,2},{4,7},{5,4},{6,5},{7,6},{8,11},{9,8},{10,9... | collective-permute-start | bytes 344072 | tf_op jit(solution)/shard_map/ppermute | solution.py:42
  185.1 1.9 partial_sums.2
  187.0 1.5 collective-permute-start.22
  188.5 2.0 collective-permute-start.23
  191.4 3.7 %collective-permute-done.22.refs_1_ = bf16[128,448]{1,0:T(8,128)(2,1)S(1)} collective-permute-done((bf16[128,448]{1,0:T(8,128)(2,1)}, bf16[128,448]{1,0:T(8,128)(2,1)S(1)}, u32[]{:S(2)}, u32[]{:S(2)}) %collective-permute-start.22) | collective-permute-done | bytes 114720 | tf_op jit(solution)/shard_map/ppermute | solution.py:46
  195.1 1.6 collective-permute-done.23.refs_2_
  197.1 0.9 final.1
  (98 shorter events, 8.6 us)
Async XLA Ops:
  7.2 3.3 %copy-start.13 = (bf16[448,64]{0,1:T(8,128)(2,1)S(1)}, bf16[448,64]{0,1:T(8,128)(2,1)}, u32[]{:S(2)}) copy-start(bf16[448,64]{0,1:T(8,128)(2,1)} %param.16) | copy-start | bytes 172036
  7.2 3.4 %copy-start.14 = (bf16[448,64]{0,1:T(8,128)(2,1)S(1)}, bf16[448,64]{0,1:T(8,128)(2,1)}, u32[]{:S(2)}) copy-start(bf16[448,64]{0,1:T(8,128)(2,1)} %param.17) | copy-start | bytes 172036
  7.2 3.6 %copy-start.12 = (bf16[448,448]{1,0:T(8,128)(2,1)S(1)}, bf16[448,448]{1,0:T(8,128)(2,1)}, u32[]{:S(2)}) copy-start(bf16[448,448]{1,0:T(8,128)(2,1)} %param.15) | copy-start | bytes 1204228
  7.2 67.4 %all-gather.5.cloned.1.call-start = ((), (), s32[]{:S(2)}) async-start(), calls=%async_computation | async-start | bytes 4734976 | tf_op jit(solution)/shard_map/all_gather | solution.py:384
  9.7 35.6 %copy-start.18 = (s32[4,64]{1,0:T(4,128)S(1)}, s32[4,64]{1,0:T(4,128)}, u32[]{:S(2)}) copy-start(s32[4,64]{1,0:T(4,128)} %param.22) | copy-start | bytes 3076
  9.7 114.2 %all-gather.7.cloned.1.call-start = ((), (), s32[]{:S(2)}) async-start(), calls=%async_computation.1 | async-start | bytes 7798784 | tf_op jit(solution)/shard_map/all_gather | solution.py:422
  10.6 49.3 %copy-start.17 = (s32[4]{0:T(128)S(1)}, s32[4]{0:T(128)}, u32[]{:S(2)}) copy-start(s32[4]{0:T(128)} %param.21) | copy-start | bytes 52
  10.9 18.9 %collective-permute-start.1 = (bf16[448,576]{1,0:T(8,128)(2,1)S(1)}, bf16[448,576]{1,0:T(8,128)(2,1)S(1)}, u32[]{:S(2)}, u32[]{:S(2)}) collective-permute-start(bf16[448,576]{1,0:T(8,128)(2,1)S(1)} %pad_maximum_fusion.refs_0_), channel_id=1, source_target_pairs={{0,32},{16,48},{32,64},{48,80},{64,96},{80,112},{96,128},{112,144}... | collective-permute-start | bytes 1548296 | tf_op jit(solution)/shard_map/ppermute | solution.py:34
  12.9 16.9 %collective-permute-start.2 = (bf16[448,576]{1,0:T(8,128)(2,1)S(1)}, bf16[448,576]{1,0:T(8,128)(2,1)S(1)}, u32[]{:S(2)}, u32[]{:S(2)}) collective-permute-start(bf16[448,576]{1,0:T(8,128)(2,1)S(1)} %pad_maximum_fusion.refs_0_), channel_id=1, source_target_pairs={{0,224},{16,240},{32,0},{48,16},{64,32},{80,48},{96,64},{112,80},{... | collective-permute-start | bytes 1548296 | tf_op jit(solution)/shard_map/ppermute | solution.py:34
  29.8 15.5 %collective-permute-start.5 = (bf16[448,576]{1,0:T(8,128)(2,1)S(1)}, bf16[448,576]{1,0:T(8,128)(2,1)S(1)}, u32[]{:S(2)}, u32[]{:S(2)}) collective-permute-start(bf16[448,576]{1,0:T(8,128)(2,1)S(1)} %collective-permute-done.1.refs_2_), channel_id=1, source_target_pairs={{0,32},{16,48},{32,64},{48,80},{64,96},{80,112},{96,128},{112,144}... | collective-permute-start | bytes 1548296 | tf_op jit(solution)/shard_map/ppermute | solution.py:34
  29.8 33.8 %collective-permute-start = (bf16[448,576]{1,0:T(8,128)(2,1)S(1)}, bf16[448,576]{1,0:T(8,128)(2,1)}, u32[]{:S(2)}, u32[]{:S(2)}) collective-permute-start(bf16[448,576]{1,0:T(8,128)(2,1)S(1)} %pad_maximum_fusion.refs_0_), channel_id=1, source_target_pairs={{0,16},{16,0},{32,48},{48,32},{64,80},{80,64},{96,112},{112,96},{1... | collective-permute-start | bytes 1548296 | tf_op jit(solution)/shard_map/ppermute | solution.py:38
  29.8 16.2 %collective-permute-start.6 = (bf16[448,576]{1,0:T(8,128)(2,1)S(1)}, bf16[448,576]{1,0:T(8,128)(2,1)}, u32[]{:S(2)}, u32[]{:S(2)}) collective-permute-start(bf16[448,576]{1,0:T(8,128)(2,1)S(1)} %collective-permute-done.2.refs_3_), channel_id=1, source_target_pairs={{0,224},{16,240},{32,0},{48,16},{64,32},{80,48},{96,64},{112,80},{... | collective-permute-start | bytes 1548296 | tf_op jit(solution)/shard_map/ppermute | solution.py:34
  45.3 14.6 %collective-permute-start.9 = (bf16[448,576]{1,0:T(8,128)(2,1)S(1)}, bf16[448,576]{1,0:T(8,128)(2,1)S(1)}, u32[]{:S(2)}, u32[]{:S(2)}) collective-permute-start(bf16[448,576]{1,0:T(8,128)(2,1)S(1)} %collective-permute-done.5.refs_6_), channel_id=1, source_target_pairs={{0,32},{16,48},{32,64},{48,80},{64,96},{80,112},{96,128},{112,144}... | collective-permute-start | bytes 1548296 | tf_op jit(solution)/shard_map/ppermute | solution.py:34
  46.1 16.1 %collective-permute-start.10 = (bf16[448,576]{1,0:T(8,128)(2,1)}, bf16[448,576]{1,0:T(8,128)(2,1)S(1)}, u32[]{:S(2)}, u32[]{:S(2)}) collective-permute-start(bf16[448,576]{1,0:T(8,128)(2,1)} %collective-permute-done.6.refs_7_), channel_id=1, source_target_pairs={{0,224},{16,240},{32,0},{48,16},{64,32},{80,48},{96,64},{112,80},{... | collective-permute-start | bytes 1548296 | tf_op jit(solution)/shard_map/ppermute | solution.py:34
  50.7 22.8 %copy-start.16 = (s32[4,8]{1,0:T(4,128)S(1)}, s32[4,8]{1,0:T(4,128)}, u32[]{:S(2)}) copy-start(s32[4,8]{1,0:T(4,128)} %param.24) | copy-start | bytes 388
  50.7 15.9 %collective-permute-start.3 = (bf16[448,576]{1,0:T(8,128)(2,1)S(1)}, bf16[448,576]{1,0:T(8,128)(2,1)}, u32[]{:S(2)}, u32[]{:S(2)}) collective-permute-start(bf16[448,576]{1,0:T(8,128)(2,1)S(1)} %collective-permute-done.1.refs_2_), channel_id=1, source_target_pairs={{0,16},{16,0},{32,48},{48,32},{64,80},{80,64},{96,112},{112,96},{1... | collective-permute-start | bytes 1548296 | tf_op jit(solution)/shard_map/ppermute | solution.py:38
  50.7 16.0 %collective-permute-start.4 = (bf16[448,576]{1,0:T(8,128)(2,1)S(1)}, bf16[448,576]{1,0:T(8,128)(2,1)}, u32[]{:S(2)}, u32[]{:S(2)}) collective-permute-start(bf16[448,576]{1,0:T(8,128)(2,1)S(1)} %collective-permute-done.2.refs_3_), channel_id=1, source_target_pairs={{0,16},{16,0},{32,48},{48,32},{64,80},{80,64},{96,112},{112,96},{1... | collective-permute-start | bytes 1548296 | tf_op jit(solution)/shard_map/ppermute | solution.py:38
  59.9 7.3 %collective-permute-start.7 = (bf16[448,576]{1,0:T(8,128)(2,1)S(1)}, bf16[448,576]{1,0:T(8,128)(2,1)}, u32[]{:S(2)}, u32[]{:S(2)}) collective-permute-start(bf16[448,576]{1,0:T(8,128)(2,1)S(1)} %collective-permute-done.5.refs_6_), channel_id=1, source_target_pairs={{0,16},{16,0},{32,48},{48,32},{64,80},{80,64},{96,112},{112,96},{1... | collective-permute-start | bytes 1548296 | tf_op jit(solution)/shard_map/ppermute | solution.py:38
  62.2 9.8 %collective-permute-start.13 = (bf16[224,576]{1,0:T(8,128)(2,1)}, bf16[224,576]{1,0:T(8,128)(2,1)}, u32[]{:S(2)}, u32[]{:S(2)}) collective-permute-start(bf16[224,576]{1,0:T(8,128)(2,1)} %slice.13), channel_id=1, source_target_pairs={{0,32},{16,48},{32,64},{48,80},{64,96},{80,112},{96,128},{112,144}... | collective-permute-start | bytes 774152 | tf_op jit(solution)/shard_map/ppermute | solution.py:34
  63.6 9.0 %collective-permute-start.14 = (bf16[224,576]{1,0:T(8,128)(2,1)}, bf16[224,576]{1,0:T(8,128)(2,1)}, u32[]{:S(2)}, u32[]{:S(2)}) collective-permute-start(bf16[224,576]{1,0:T(8,128)(2,1)} %slice.14), channel_id=1, source_target_pairs={{0,224},{16,240},{32,0},{48,16},{64,32},{80,48},{96,64},{112,80},{... | collective-permute-start | bytes 774152 | tf_op jit(solution)/shard_map/ppermute | solution.py:34
  66.7 7.0 %collective-permute-start.8 = (bf16[448,576]{1,0:T(8,128)(2,1)}, bf16[448,576]{1,0:T(8,128)(2,1)}, u32[]{:S(2)}, u32[]{:S(2)}) collective-permute-start(bf16[448,576]{1,0:T(8,128)(2,1)} %collective-permute-done.6.refs_7_), channel_id=1, source_target_pairs={{0,16},{16,0},{32,48},{48,32},{64,80},{80,64},{96,112},{112,96},{1... | collective-permute-start | bytes 1548296 | tf_op jit(solution)/shard_map/ppermute | solution.py:38
  66.7 7.9 %collective-permute-start.11 = (bf16[448,576]{1,0:T(8,128)(2,1)S(1)}, bf16[448,576]{1,0:T(8,128)(2,1)}, u32[]{:S(2)}, u32[]{:S(2)}) collective-permute-start(bf16[448,576]{1,0:T(8,128)(2,1)S(1)} %collective-permute-done.9.refs_10_), channel_id=1, source_target_pairs={{0,16},{16,0},{32,48},{48,32},{64,80},{80,64},{96,112},{112,96},{1... | collective-permute-start | bytes 1548296 | tf_op jit(solution)/shard_map/ppermute | solution.py:38
  67.2 7.4 %collective-permute-start.12 = (bf16[448,576]{1,0:T(8,128)(2,1)S(1)}, bf16[448,576]{1,0:T(8,128)(2,1)}, u32[]{:S(2)}, u32[]{:S(2)}) collective-permute-start(bf16[448,576]{1,0:T(8,128)(2,1)S(1)} %collective-permute-done.10.refs_11_), channel_id=1, source_target_pairs={{0,16},{16,0},{32,48},{48,32},{64,80},{80,64},{96,112},{112,96},{1... | collective-permute-start | bytes 1548296 | tf_op jit(solution)/shard_map/ppermute | solution.py:38
  72.1 1.9 collective-permute-start.15
  72.6 1.9 collective-permute-start.16
  76.8 17.6 %copy-start.2 = (bf16[4,1,1,2048,128]{4,3,2,1,0:T(8,128)(2,1)S(1)}, bf16[4,1,1,2048,128]{4,3,2,1,0:T(8,128)(2,1)}, u32[]{:S(2)}) copy-start(bf16[4,1,1,2048,128]{4,3,2,1,0:T(8,128)(2,1)} %param.19) | copy-start | bytes 6291460
  76.8 17.6 %copy-start.3 = (bf16[4,1,1,2048,128]{4,3,2,1,0:T(8,128)(2,1)S(1)}, bf16[4,1,1,2048,128]{4,3,2,1,0:T(8,128)(2,1)}, u32[]{:S(2)}) copy-start(bf16[4,1,1,2048,128]{4,3,2,1,0:T(8,128)(2,1)} %param.20) | copy-start | bytes 6291460
  76.8 17.6 %copy-start.5 = (f32[256,128]{1,0:T(8,128)S(1)}, f32[256,128]{1,0:T(8,128)}, u32[]{:S(2)}) copy-start(f32[256,128]{1,0:T(8,128)} %get-tuple-element.49.cos_ref) | copy-start | bytes 393220
  76.9 17.6 %copy-start.6 = (f32[256,128]{1,0:T(8,128)S(1)}, f32[256,128]{1,0:T(8,128)}, u32[]{:S(2)}) copy-start(f32[256,128]{1,0:T(8,128)} %get-tuple-element.50.sin_ref) | copy-start | bytes 393220
  76.9 17.6 %copy-start.7 = (f32[4,64,64]{2,1,0:T(8,128)S(1)}, f32[4,64,64]{2,1,0:T(8,128)}, u32[]{:S(2)}) copy-start(f32[4,64,64]{2,1,0:T(8,128)} %get-tuple-element.48.reach_ref) | copy-start | bytes 196612
  84.6 9.8 %collective-permute-start.17 = (bf16[256,576]{1,0:T(8,128)(2,1)S(1)}, bf16[256,576]{1,0:T(8,128)(2,1)S(1)}, u32[]{:S(2)}, u32[]{:S(2)}) collective-permute-start(bf16[256,576]{1,0:T(8,128)(2,1)S(1)} %project.1.own_ref), channel_id=1, source_target_pairs={{0,1},{1,0},{2,3},{3,2},{4,5},{5,4},{6,7},{7,6},{8,9},{9,8},{10,11... | collective-permute-start | bytes 884744 | tf_op jit(solution)/shard_map/ppermute | solution.py:50
  94.5 16.7 %copy-start.15 = (s32[4,64]{1,0:T(4,128)S(1)}, s32[4,64]{1,0:T(4,128)}, u32[]{:S(2)}) copy-start(s32[4,64]{1,0:T(4,128)} %param.23) | copy-start | bytes 3076
  111.0 6.5 %collective-permute-start.18 = (bf16[256,512]{1,0:T(8,128)(2,1)S(1)}, bf16[256,512]{1,0:T(8,128)(2,1)S(1)}, u32[]{:S(2)}, u32[]{:S(2)}) collective-permute-start(bf16[256,512]{1,0:T(8,128)(2,1)S(1)} %get-tuple-element.24), channel_id=1, source_target_pairs={{0,1},{1,0},{2,3},{3,2},{4,5},{5,4},{6,7},{7,6},{8,9},{9,8},{10,11... | collective-permute-start | bytes 786440 | tf_op jit(solution)/shard_map/ppermute | solution.py:50
  128.8 26.6 %collective-permute-start.27 = (bf16[4,128,448]{2,1,0:T(8,128)(2,1)S(1)}, bf16[4,128,448]{2,1,0:T(8,128)(2,1)S(1)}, u32[]{:S(2)}, u32[]{:S(2)}) collective-permute-start(bf16[4,128,448]{2,1,0:T(8,128)(2,1)S(1)} %get-tuple-element.36), channel_id=1, source_target_pairs={{0,12},{1,13},{2,14},{3,15},{4,0},{5,1},{6,2},{7,3},{8,4},{9,5},{1... | collective-permute-start | bytes 1376264 | tf_op jit(solution)/shard_map/ppermute | solution.py:46
  132.6 25.1 %collective-permute-start.25 = (bf16[4,128,448]{2,1,0:T(8,128)(2,1)}, bf16[4,128,448]{2,1,0:T(8,128)(2,1)}, u32[]{:S(2)}, u32[]{:S(2)}) collective-permute-start(bf16[4,128,448]{2,1,0:T(8,128)(2,1)} %get-tuple-element.34), channel_id=1, source_target_pairs={{0,8},{1,9},{2,10},{3,11},{4,12},{5,13},{6,14},{7,15},{8,0},{9,1},... | collective-permute-start | bytes 1376264 | tf_op jit(solution)/shard_map/ppermute | solution.py:46
  133.7 25.5 %collective-permute-start.26 = (bf16[4,128,448]{2,1,0:T(8,128)(2,1)}, bf16[4,128,448]{2,1,0:T(8,128)(2,1)}, u32[]{:S(2)}, u32[]{:S(2)}) collective-permute-start(bf16[4,128,448]{2,1,0:T(8,128)(2,1)} %get-tuple-element.35), channel_id=1, source_target_pairs={{0,4},{1,5},{2,6},{3,7},{4,8},{5,9},{6,10},{7,11},{8,12},{9,13},{1... | collective-permute-start | bytes 1376264 | tf_op jit(solution)/shard_map/ppermute | solution.py:46
  135.8 46.5 %collective-permute-start.21 = (bf16[4,128,448]{2,1,0:T(8,128)(2,1)}, bf16[4,128,448]{2,1,0:T(8,128)(2,1)S(1)}, u32[]{:S(2)}, u32[]{:S(2)}) collective-permute-start(bf16[4,128,448]{2,1,0:T(8,128)(2,1)} %get-tuple-element.28), channel_id=1, source_target_pairs={{0,3},{1,0},{2,1},{3,2},{4,7},{5,4},{6,5},{7,6},{8,11},{9,8},{10,9... | collective-permute-start | bytes 1376264 | tf_op jit(solution)/shard_map/ppermute | solution.py:42
  138.6 46.5 %collective-permute-start.19 = (bf16[4,128,448]{2,1,0:T(8,128)(2,1)}, bf16[4,128,448]{2,1,0:T(8,128)(2,1)S(1)}, u32[]{:S(2)}, u32[]{:S(2)}) collective-permute-start(bf16[4,128,448]{2,1,0:T(8,128)(2,1)} %get-tuple-element.26), channel_id=1, source_target_pairs={{0,2},{1,3},{2,0},{3,1},{4,6},{5,7},{6,4},{7,5},{8,10},{9,11},{10,... | collective-permute-start | bytes 1376264 | tf_op jit(solution)/shard_map/ppermute | solution.py:42
  156.2 28.8 %collective-permute-start.20 = (bf16[4,128,448]{2,1,0:T(8,128)(2,1)}, bf16[4,128,448]{2,1,0:T(8,128)(2,1)}, u32[]{:S(2)}, u32[]{:S(2)}) collective-permute-start(bf16[4,128,448]{2,1,0:T(8,128)(2,1)} %get-tuple-element.27), channel_id=1, source_target_pairs={{0,1},{1,2},{2,3},{3,0},{4,5},{5,6},{6,7},{7,4},{8,9},{9,10},{10,1... | collective-permute-start | bytes 1376264 | tf_op jit(solution)/shard_map/ppermute | solution.py:42
  163.0 27.5 %collective-permute-start.28 = (bf16[128,448]{1,0:T(8,128)(2,1)S(1)}, bf16[128,448]{1,0:T(8,128)(2,1)S(1)}, u32[]{:S(2)}, u32[]{:S(2)}) collective-permute-start(bf16[128,448]{1,0:T(8,128)(2,1)S(1)} %get-tuple-element.38), channel_id=1, source_target_pairs={{0,2},{1,3},{2,0},{3,1},{4,6},{5,7},{6,4},{7,5},{8,10},{9,11},{10,... | collective-permute-start | bytes 344072 | tf_op jit(solution)/shard_map/ppermute | solution.py:42
  181.8 9.6 %collective-permute-start.29 = (bf16[128,448]{1,0:T(8,128)(2,1)}, bf16[128,448]{1,0:T(8,128)(2,1)S(1)}, u32[]{:S(2)}, u32[]{:S(2)}) collective-permute-start(bf16[128,448]{1,0:T(8,128)(2,1)} %get-tuple-element.39), channel_id=1, source_target_pairs={{0,1},{1,2},{2,3},{3,0},{4,5},{5,6},{6,7},{7,4},{8,9},{9,10},{10,1... | collective-permute-start | bytes 344072 | tf_op jit(solution)/shard_map/ppermute | solution.py:42
  182.4 9.0 %collective-permute-start.30 = (bf16[128,448]{1,0:T(8,128)(2,1)S(1)}, bf16[128,448]{1,0:T(8,128)(2,1)S(1)}, u32[]{:S(2)}, u32[]{:S(2)}) collective-permute-start(bf16[128,448]{1,0:T(8,128)(2,1)S(1)} %get-tuple-element.40), channel_id=1, source_target_pairs={{0,3},{1,0},{2,1},{3,2},{4,7},{5,4},{6,5},{7,6},{8,11},{9,8},{10,9... | collective-permute-start | bytes 344072 | tf_op jit(solution)/shard_map/ppermute | solution.py:42
  185.1 5.5 %copy-start.19 = (s32[64]{0:T(128)S(1)}, s32[64]{0:T(128)}, u32[]{:S(2)}) copy-start(s32[64]{0:T(128)} %param.25) | copy-start | bytes 772
  185.1 12.1 %copy-start.4 = (bf16[4,64,448]{2,1,0:T(8,128)(2,1)S(1)}, bf16[4,64,448]{2,1,0:T(8,128)(2,1)}, u32[]{:S(2)}) copy-start(bf16[4,64,448]{2,1,0:T(8,128)(2,1)} %param.13) | copy-start | bytes 688132
  185.1 12.1 %copy-start.11 = (f32[128,448]{1,0:T(8,128)S(1)}, f32[128,448]{1,0:T(8,128)}, u32[]{:S(2)}) copy-start(f32[128,448]{1,0:T(8,128)} %copy-done.10) | copy-start | bytes 688132
  187.0 8.1 %collective-permute-start.22 = (bf16[128,448]{1,0:T(8,128)(2,1)}, bf16[128,448]{1,0:T(8,128)(2,1)S(1)}, u32[]{:S(2)}, u32[]{:S(2)}) collective-permute-start(bf16[128,448]{1,0:T(8,128)(2,1)} %get-tuple-element.30), channel_id=1, source_target_pairs={{0,8},{1,9},{2,10},{3,11},{4,12},{5,13},{6,14},{7,15},{8,0},{9,1},... | collective-permute-start | bytes 344072 | tf_op jit(solution)/shard_map/ppermute | solution.py:46
  188.5 8.2 %collective-permute-start.23 = (bf16[128,448]{1,0:T(8,128)(2,1)}, bf16[128,448]{1,0:T(8,128)(2,1)S(1)}, u32[]{:S(2)}, u32[]{:S(2)}) collective-permute-start(bf16[128,448]{1,0:T(8,128)(2,1)} %get-tuple-element.31), channel_id=1, source_target_pairs={{0,4},{1,5},{2,6},{3,7},{4,8},{5,9},{6,10},{7,11},{8,12},{9,13},{1... | collective-permute-start | bytes 344072 | tf_op jit(solution)/shard_map/ppermute | solution.py:46
  190.5 6.6 %collective-permute-start.24 = (bf16[128,448]{1,0:T(8,128)(2,1)S(1)}, bf16[128,448]{1,0:T(8,128)(2,1)S(1)}, u32[]{:S(2)}, u32[]{:S(2)}) collective-permute-start(bf16[128,448]{1,0:T(8,128)(2,1)S(1)} %get-tuple-element.32), channel_id=1, source_target_pairs={{0,12},{1,13},{2,14},{3,15},{4,0},{5,1},{6,2},{7,3},{8,4},{9,5},{1... | collective-permute-start | bytes 344072 | tf_op jit(solution)/shard_map/ppermute | solution.py:46
  (5 other events, 7.9 us)
Sparse Core Ops, SparseCore 0:
  10.5 60.7 all-gather.4
  73.1 50.7 all-gather.6
